TPU v7x, 32 devices: a whole 2x2x4 slice. The times are simulated.
32 devices in a mesh: grp: 1, var: 4 (over z), smp: 4 (over y, x), sub: 2 (over core).
Axes of the slice: x: 2, y: 2, z: 4, core: 2. Of those that a mesh axis runs over, the one named last changes fastest.
Arguments:
- dosages: bfloat16 [4096, 1024], P(('smp', 'sub'), ('grp', 'var')), may hold values from 0 to 2
- reach_blk: int32 [8], P('grp'), may hold values from 0 to 12, as said below
- locus_start: int32 [32], P('grp'), may hold values from 0 to 7
- locus_end: int32 [32], P('grp'), may hold values from 0 to 7, as said below
- locus_effects: bfloat16 [32, 1024], P(('grp', 'var', 'smp', 'sub')), may hold values from -6 to 6
Outputs:
- locus_scores: float32 [32, 1024], P(('grp', 'var', 'smp', 'sub'))
Inputs may be any that keep to these rules, and one draw needn't show every extreme that they name: `reach_blk`: every value from 0 to 12 may occur, and 12 occurs in every draw. locus_end - locus_start + 1 lies in 1 to 8, and is 8 for some locus in every draw; loci may intersect one another.
All inputs are finite; a program needn't handle non-finite values.
Results may differ from a plain program's by a relative error of at most 0.0003.
Values may be sent and summed in bfloat16 or wider, within the bound.
A program may use at most 64 MiB of HBM per device.

v0:
```python
import jax
import jax.numpy as jnp
from jax import lax
from jax.sharding import PartitionSpec as P

BLK = 128
REACH = 12
LMAX = 8


EPS = 1e-05
HIGHEST = lax.Precision.HIGHEST


def shifted(block, axis, distance):
    devices = range(lax.axis_size(axis))
    route = [(i - distance, i) for i in devices if i - distance in devices]
    return lax.ppermute(block, axis, route)


def slot_table(locus_start, locus_end, first_blk, window_blocks):
    lengths = locus_end - locus_start + 1
    slot_ids = jnp.arange(LMAX, dtype=jnp.int32)
    target = locus_start[:, None] + slot_ids[None, :] - first_blk
    live_slot = slot_ids[None, :] < lengths[:, None]
    blocks = jnp.arange(window_blocks, dtype=jnp.int32)
    hits = live_slot[:, :, None] & (target[:, :, None] == blocks[None, None, :])
    return jnp.where(hits, 1.0, 0.0).astype(jnp.float32)


def fetch_ahead(dosages, halo_cols):
    stripe = dosages.shape[1]
    hops = (halo_cols + stripe - 1) // stripe
    pieces = [dosages]
    for distance in range(1, hops + 1):
        pieces.append(shifted(dosages, "var", -distance))
    joined = jnp.concatenate(pieces, axis=1)
    return joined


def body(dosages, reach_blk, locus_start, locus_end, locus_effects):
    row_local, stripe = dosages.shape
    block_count = reach_blk.shape[0]
    locus_count = locus_start.shape[0]
    halo_cols = REACH * BLK
    window = fetch_ahead(dosages, halo_cols)
    win_cols = window.shape[1]
    shards = lax.axis_size(("smp", "sub"))
    samples = row_local * shards
    col_sum = lax.psum(jnp.sum(window, axis=0, dtype=jnp.float32), ("smp", "sub"))
    col_mean = col_sum / samples
    centred = jnp.sum(jnp.square(window.astype(jnp.float32) - col_mean[None, :]), axis=0)
    spread = lax.psum(centred, ("smp", "sub"))
    inv_sd = lax.rsqrt(spread / samples + EPS)
    cross_prod = lax.dot_general(
        dosages, window, (((0,), (0,)), ((), ())), preferred_element_type=jnp.float32
    )
    row_first = jnp.int32(0)
    ld_corr = (cross_prod / samples - col_mean[:stripe, None] * col_mean[None, :] / shards) * (
        inv_sd[:stripe, None] * inv_sd[None, :]
    )
    stripe_blocks = stripe // BLK
    first_blk = lax.axis_index("var") * stripe_blocks
    reach_local = lax.dynamic_slice_in_dim(reach_blk, first_blk, stripe_blocks)
    row_blocks = jnp.arange(stripe, dtype=jnp.int32) // BLK
    stripe_ids = jnp.arange(stripe_blocks, dtype=jnp.int32)
    reach_rows = jnp.sum(
        jnp.where(row_blocks[:, None] == stripe_ids[None, :], reach_local[None, :], 0), axis=1
    )
    col_blocks = jnp.arange(win_cols, dtype=jnp.int32) // BLK
    block_gap = col_blocks[None, :] - row_blocks[:, None]
    keep_mask = (
        (block_gap >= 0)
        & (block_gap <= reach_rows[:, None])
        & (first_blk + col_blocks[None, :] < block_count)
    )
    band_corr = jnp.where(keep_mask, ld_corr, 0.0)
    strict = jnp.where(block_gap > 0, band_corr, 0.0)
    window_blocks = win_cols // BLK
    lookup = slot_table(locus_start, locus_end, first_blk, window_blocks)
    gathered = lax.all_gather(locus_effects, ("var", "smp", "sub"), axis=0, tiled=True)
    effects = gathered.astype(jnp.float32).reshape(locus_count, LMAX, BLK)
    b_window = jnp.einsum("lkw,lkc->lwc", lookup, effects, precision=HIGHEST).reshape(
        locus_count, win_cols
    )
    b_rows = lax.dynamic_slice_in_dim(b_window, row_first, stripe, 1)
    y_rows = jnp.dot(b_window, band_corr.T, precision=HIGHEST)
    y_cols = jnp.dot(b_rows, strict, precision=HIGHEST)
    y_window = y_cols + lax.dynamic_update_slice_in_dim(
        jnp.zeros_like(y_cols), y_rows, row_first, 1
    )
    scores = jnp.einsum(
        "lkw,lwc->lkc", lookup, y_window.reshape(locus_count, window_blocks, BLK), precision=HIGHEST
    )
    return lax.psum_scatter(
        scores.reshape(locus_count, LMAX * BLK),
        ("var", "smp", "sub"),
        scatter_dimension=0,
        tiled=True,
    )


def solution(mesh):
    in_specs = (
        P(("smp", "sub"), ("grp", "var")),
        P("grp"),
        P("grp"),
        P("grp"),
        P(("grp", "var", "smp", "sub"), None),
    )
    out_specs = P(("grp", "var", "smp", "sub"), None)
    return jax.shard_map(body, mesh=mesh, in_specs=in_specs, out_specs=out_specs, check_vma=False)
```

profile of v0, /device:TPU:0, one launch (start us, length us, event | category | flops | bytes accessed | tf_op | source)
XLA Modules:
  0.0 226.5 jit_solution(7181210904533496938)
XLA Ops:
  6.5 0.0 all-reduce.4.cloned.1.call-start
  6.5 1.3 collective-permute-start
  7.8 1.3 collective-permute-start.1
  9.1 1.3 collective-permute-start.2
  10.4 0.7 collective-permute-start.3
  11.1 1.0 constant_dynamic-update-slice_fusion.6
  12.1 49.6 %all-gather = bf16[32,1,1024]{2,1,0:T(2,128)(2,1)S(1)} all-gather(bf16[1,1,1024]{2,1,0:T(2,128)(2,1)} %bitcast.32), channel_id=1, replica_groups=mesh['grp'=1,'var'=4,'smp'=4,'sub'=2] {'var','smp','sub'}, dimensions={0}, use_global_device_ids=true | all-gather | bytes 67584 | tf_op jit(solution)/shard_map/all_gather | solution.py:81
  61.7 0.4 reduce
  62.1 0.7 add_subtract_fusion
  62.8 0.7 subtract_add_fusion
  63.5 0.1 iota_compare_fusion.1
  63.6 0.7 dynamic_slice.7
  64.3 0.5 fusion.15
  64.9 0.1 fusion.32
  65.0 0.1 copy.11
  65.0 0.0 collective-permute-done
  65.1 0.0 collective-permute-done.1
  65.1 0.0 collective-permute-done.2
  65.2 0.0 collective-permute-done.3
  65.3 0.0 copy-start
  65.3 0.3 convert_reduce_fusion
  65.6 12.2 %psum.14 = f32[1792]{0:T(1024)S(1)} all-reduce(f32[1792]{0:T(1024)S(1)} %convert_reduce_fusion), channel_id=1, replica_groups=mesh['grp'=1,'var'=4,'smp'=4,'sub'=2] {'smp','sub'}, use_global_device_ids=true, to_apply=%region_2.0 | all-reduce | flops 1792 | bytes 14336 | tf_op jit(solution)/shard_map/psum | solution.py:50
  77.8 0.5 fusion.1
  78.3 12.0 %psum.15 = f32[1792]{0:T(1024)S(1)} all-reduce(f32[1792]{0:T(1024)S(1)} %fusion.1), channel_id=1, replica_groups=mesh['grp'=1,'var'=4,'smp'=4,'sub'=2] {'smp','sub'}, use_global_device_ids=true, to_apply=%region_4.5 | all-reduce | flops 1792 | bytes 14336 | tf_op jit(solution)/shard_map/psum | solution.py:53
  90.4 0.0 copy-done
  90.4 1.6 fusion.5
  92.0 1.0 fusion.39
  92.9 1.9 convolution_add_fusion
  94.9 0.4 fusion.13
  95.3 0.7 copy.12
  96.0 0.0 all-reduce.4.cloned.1.call-update
  96.0 122.3 %all-reduce.4.cloned.1.call-done = f32[32,1024]{1,0:T(8,128)} async-done(((f32[32,1024]{1,0:T(8,128)}), f32[32,1024]{1,0:T(8,128)}) %all-reduce.4.cloned.1.call-update) | async-done | bytes 131088
  218.3 1.4 constant_dynamic-slice_fusion
  (15 shorter events, 0.2 us)
Async XLA Ops:
  6.5 211.8 %all-reduce.4.cloned.1.call-start = ((), (), s32[]{:S(2)}) async-start(), calls=%async_computation | async-start | bytes 262144
  6.5 58.5 %collective-permute-start = (bf16[512,256]{1,0:T(8,128)(2,1)}, bf16[512,256]{1,0:T(8,128)(2,1)S(1)}, u32[]{:S(2)}, u32[]{:S(2)}) collective-permute-start(bf16[512,256]{1,0:T(8,128)(2,1)} %param.5), channel_id=1, source_target_pairs={{8,0},{16,8},{24,16},{9,1},{17,9},{25,17},{10,2},{18,10},{26,18},{... | collective-permute-start | bytes 786440 | tf_op jit(solution)/shard_map/ppermute | solution.py:18
  7.8 57.3 %collective-permute-start.1 = (bf16[512,256]{1,0:T(8,128)(2,1)}, bf16[512,256]{1,0:T(8,128)(2,1)S(1)}, u32[]{:S(2)}, u32[]{:S(2)}) collective-permute-start(bf16[512,256]{1,0:T(8,128)(2,1)} %param.5), channel_id=1, source_target_pairs={{16,0},{24,8},{17,1},{25,9},{18,2},{26,10},{19,3},{27,11},{20,4},{... | collective-permute-start | bytes 786440 | tf_op jit(solution)/shard_map/ppermute | solution.py:18
  9.1 56.0 %collective-permute-start.2 = (bf16[512,256]{1,0:T(8,128)(2,1)}, bf16[512,256]{1,0:T(8,128)(2,1)S(1)}, u32[]{:S(2)}, u32[]{:S(2)}) collective-permute-start(bf16[512,256]{1,0:T(8,128)(2,1)} %param.5), channel_id=1, source_target_pairs={{24,0},{25,1},{26,2},{27,3},{28,4},{29,5},{30,6},{31,7}} | collective-permute-start | bytes 786440 | tf_op jit(solution)/shard_map/ppermute | solution.py:18
  10.4 54.7 %collective-permute-start.3 = (bf16[512,256]{1,0:T(8,128)(2,1)}, bf16[512,256]{1,0:T(8,128)(2,1)S(1)}, u32[]{:S(2)}, u32[]{:S(2)}) collective-permute-start(bf16[512,256]{1,0:T(8,128)(2,1)} %param.5), channel_id=1, source_target_pairs={} | collective-permute-start | bytes 786440 | tf_op jit(solution)/shard_map/ppermute | solution.py:18
  65.3 25.1 %copy-start = (bf16[512,256]{1,0:T(8,128)(2,1)S(1)}, bf16[512,256]{1,0:T(8,128)(2,1)}, u32[]{:S(2)}) copy-start(bf16[512,256]{1,0:T(8,128)(2,1)} %param.5) | copy-start | bytes 786436
Sparse Core Ops, SparseCore 0:
  96.2 122.1 all-reduce.3
where the time goes:
time: 227 us
  waiting for transfers between devices  122 us (54%)
  blocking collectives  73.9 us (33%)
  between operations  13.6 us (6%)
  matrix products  5.4 us (2%)
  starting transfers between devices  4.54 us (2%)
  local copies, waits for them, and re-layouts  3.99 us (2%)
  other arithmetic  2.79 us (1%)
    unnamed x2, waiting for transfers between devices  122 us
    all_gather x1, blocking collectives, body(): lax.all_gather(locus_effects, ('var', 'smp', 'sub'), axis=0, tiled=True)  49.6 us
    psum x1, blocking collectives, body(): lax.psum(jnp.sum(window, axis=0, dtype=jnp.float32), ('smp', 'sub'))  12.2 us
    psum x1, blocking collectives, body(): spread = lax.psum(centred, ('smp', 'sub'))  12 us
  transfers between devices with their start and end apart: 5, of which 1 were waited for; matrix products, arithmetic and copies ran while one was open for 2% of the time, Pallas kernels for 0%

commit v1 on v0

--- a/solution.py
+++ b/solution.py
@@ -1,6 +1,10 @@
+import functools
+
 import jax
 import jax.numpy as jnp
 from jax import lax
+from jax.experimental import pallas as pl
+from jax.experimental.pallas import tpu as pltpu
 from jax.sharding import PartitionSpec as P
 
 BLK = 128
@@ -38,7 +42,7 @@
     return joined
 
 
-def body(dosages, reach_blk, locus_start, locus_end, locus_effects):
+def wide_body(dosages, reach_blk, locus_start, locus_end, locus_effects):
     row_local, stripe = dosages.shape
     block_count = reach_blk.shape[0]
     locus_count = locus_start.shape[0]
@@ -100,6 +104,208 @@
     )
 
 
+MESH = pl.DeviceIdType.MESH
+
+
+def halves(values):
+    high = values.astype(jnp.bfloat16)
+    low = (values - high.astype(jnp.float32)).astype(jnp.bfloat16)
+    return jnp.concatenate([high, low], axis=0)
+
+
+def kernel(n_var, n_smp, n_sub, dos_any, reach, start, end, eff_ref, out_ref,
+           local, x, st, ms, e, y, ry, rs, rz,
+           local_sem, x_s, x_r, st_s, st_r, ms_s, ms_r, e1_s, e1_r, e2_s, e2_r,
+           ry_s, ry_r, rz_s, rz_r):
+    n_pl = n_smp * n_sub
+    rows, stripe = dos_any.shape
+    part = rows // n_var
+    per_stripe = stripe // BLK
+    blocks = n_var * per_stripe
+    loci = n_var * n_pl
+    samples = rows * n_pl
+    v = lax.axis_index("var")
+    p = lax.axis_index("smp") * n_sub + lax.axis_index("sub")
+
+    def var_peer(d):
+        t = lax.rem(v + d, n_var)
+        return t, {"var": t}
+
+    def plane_peer(d):
+        q = lax.rem(p + d, n_pl)
+        return q, {"smp": lax.div(q, n_sub), "sub": lax.rem(q, n_sub)}
+
+    def rows_of(index, count):
+        return pl.ds(pl.multiple_of(index * count, count), count)
+
+    def send(src, dst, s_sem, r_sem, peer):
+        copy = pltpu.make_async_remote_copy(
+            src_ref=src, dst_ref=dst, send_sem=s_sem, recv_sem=r_sem,
+            device_id=peer, device_id_type=MESH)
+        copy.start()
+        return copy
+
+    whole = pltpu.make_async_copy(dos_any, local, local_sem.at[0])
+    whole.start()
+    own = pltpu.make_async_copy(dos_any.at[rows_of(v, part), :], x.at[v], local_sem.at[1])
+    own.start()
+
+    barrier = pltpu.get_barrier_semaphore()
+    for d in range(1, n_var):
+        pl.semaphore_signal(barrier, inc=1, device_id=var_peer(d)[1], device_id_type=MESH)
+    for d in range(1, n_pl):
+        pl.semaphore_signal(barrier, inc=1, device_id=plane_peer(d)[1], device_id_type=MESH)
+
+    me = v * n_pl + p
+    first, last = start[me], end[me]
+    block_row = lax.broadcasted_iota(jnp.int32, (blocks, BLK), 0)
+    eff = eff_ref[...].astype(jnp.float32)
+    placed = jnp.zeros((blocks, BLK), jnp.float32)
+    for k in range(eff.shape[1] // BLK):
+        hit = (block_row == first + k) & (block_row <= last)
+        placed = placed + jnp.where(hit, eff[:, k * BLK:(k + 1) * BLK], 0.0)
+    own_rows = rows_of(p * n_var + v, blocks)
+    e[own_rows, :] = placed
+
+    pl.semaphore_wait(barrier, n_var - 1 + n_pl - 1)
+    e1 = [send(e.at[own_rows, :], e.at[own_rows, :], e1_s.at[d], e1_r.at[d], var_peer(d)[1])
+          for d in range(1, n_var)]
+    xs = []
+    for d in range(1, n_var):
+        t, peer = var_peer(d)
+        xs.append(send(dos_any.at[rows_of(t, part), :], x.at[v], x_s.at[d], x_r.at[d], peer))
+
+    whole.wait()
+    mine = local[...].astype(jnp.float32)
+    total = jnp.sum(mine, axis=0, keepdims=True)
+    sq = jnp.sum(jnp.square(mine - total / rows), axis=0, keepdims=True)
+    st[p, 0:1, :] = total
+    st[p, 1:2, :] = sq
+    sts = [send(st.at[p], st.at[p], st_s.at[d], st_r.at[d], plane_peer(d)[1])
+           for d in range(1, n_pl)]
+
+    for copy in e1:
+        copy.wait()
+    group = rows_of(p, n_var * blocks)
+    e2 = [send(e.at[group, :], e.at[group, :], e2_s.at[d], e2_r.at[d], plane_peer(d)[1])
+          for d in range(1, n_pl)]
+
+    for copy in sts:
+        copy.wait()
+    mean = st[0, 0:1, :]
+    for q in range(1, n_pl):
+        mean = mean + st[q, 0:1, :]
+    mean = mean / samples
+    spread = jnp.zeros_like(mean)
+    for q in range(n_pl):
+        spread = spread + (st[q, 1:2, :] + rows * jnp.square(st[q, 0:1, :] / rows - mean))
+    ms[v, 0:1, :] = mean
+    ms[v, 1:2, :] = lax.rsqrt(spread / samples + EPS)
+    mss = [send(ms.at[v], ms.at[v], ms_s.at[d], ms_r.at[d], var_peer(d)[1])
+           for d in range(1, n_var)]
+    for copy in e2:
+        copy.wait()
+    for copy in mss:
+        copy.wait()
+    own.wait()
+    for copy in xs:
+        copy.wait()
+
+    def cols(j):
+        return j // per_stripe, slice((j % per_stripe) * BLK, (j % per_stripe + 1) * BLK)
+
+    parts = []
+    for j in range(blocks):
+        s, c = cols(j)
+        z = e[pl.ds(j, loci, stride=blocks), :] * ms[s, 1:2, c]
+        w = lax.dot_general(halves(z), x[s, :, c], (((1,), (1,)), ((), ())),
+                            preferred_element_type=jnp.float32)
+        shift = jnp.sum(z * ms[s, 0:1, c], axis=1, keepdims=True)
+        parts.append(w[:loci] + w[loci:] - shift)
+    for i in range(blocks):
+        s, c = cols(i)
+        summed = parts[i]
+        for j in range(blocks):
+            if j != i:
+                low, high = min(i, j), max(i, j)
+                summed = summed + jnp.where(reach[low] >= high - low, 1.0, 0.0) * parts[j]
+        r = lax.dot_general(halves(summed), x[s, :, c], (((1,), (0,)), ((), ())),
+                            preferred_element_type=jnp.float32)
+        y[pl.ds(i, loci, stride=blocks), :] = (r[:loci] + r[loci:]) * (ms[s, 1:2, c] / samples)
+
+    rys = []
+    for d in range(1, n_pl):
+        q, peer = plane_peer(d)
+        rys.append(send(y.at[rows_of(q, n_var * blocks), :], ry.at[p], ry_s.at[d], ry_r.at[d], peer))
+    ry[p] = y[group, :]
+    for copy in rys:
+        copy.wait()
+    acc = ry[0]
+    for q in range(1, n_pl):
+        acc = acc + ry[q]
+    rs[...] = acc
+    rzs = []
+    for d in range(1, n_var):
+        t, peer = var_peer(d)
+        rzs.append(send(rs.at[rows_of(t, blocks), :], rz.at[v], rz_s.at[d], rz_r.at[d], peer))
+    rz[v] = rs[rows_of(v, blocks), :]
+    for copy in rzs:
+        copy.wait()
+    score = rz[0]
+    for t in range(1, n_var):
+        score = score + rz[t]
+    for k in range(eff.shape[1] // BLK):
+        hit = (block_row == first + k) & (block_row <= last)
+        out_ref[:, k * BLK:(k + 1) * BLK] = jnp.sum(jnp.where(hit, score, 0.0), axis=0, keepdims=True)
+
+
+def slab_body(dosages, reach_blk, locus_start, locus_end, locus_effects):
+    n_var, n_smp, n_sub = (lax.axis_size(a) for a in ("var", "smp", "sub"))
+    n_pl = n_smp * n_sub
+    rows, stripe = dosages.shape
+    blocks = reach_blk.shape[0]
+    loci = locus_start.shape[0]
+    f32 = jnp.float32
+    dma = pltpu.SemaphoreType.DMA
+    smem = pl.BlockSpec(memory_space=pltpu.SMEM)
+    vmem = pl.BlockSpec(memory_space=pltpu.VMEM)
+    return pl.pallas_call(
+        functools.partial(kernel, n_var, n_smp, n_sub),
+        out_shape=jax.ShapeDtypeStruct(locus_effects.shape, f32),
+        in_specs=[pl.BlockSpec(memory_space=pl.ANY), smem, smem, smem, vmem],
+        out_specs=vmem,
+        scratch_shapes=[
+            pltpu.VMEM((rows, stripe), dosages.dtype),
+            pltpu.VMEM((n_var, rows // n_var, stripe), dosages.dtype),
+            pltpu.VMEM((n_pl, 2, stripe), f32),
+            pltpu.VMEM((n_var, 2, stripe), f32),
+            pltpu.VMEM((loci * blocks, BLK), f32),
+            pltpu.VMEM((loci * blocks, BLK), f32),
+            pltpu.VMEM((n_pl, n_var * blocks, BLK), f32),
+            pltpu.VMEM((n_var * blocks, BLK), f32),
+            pltpu.VMEM((n_var, blocks, BLK), f32),
+            dma((2,)),
+            dma((n_var,)), dma((n_var,)),
+            dma((n_pl,)), dma((n_pl,)),
+            dma((n_var,)), dma((n_var,)),
+            dma((n_var,)), dma((n_var,)),
+            dma((n_pl,)), dma((n_pl,)),
+            dma((n_pl,)), dma((n_pl,)),
+            dma((n_var,)), dma((n_var,)),
+        ],
+        compiler_params=pltpu.CompilerParams(
+            collective_id=0, has_side_effects=True, vmem_limit_bytes=16 * 1024 * 1024),
+    )(dosages, reach_blk, locus_start, locus_end, locus_effects)
+
+
+def body(dosages, reach_blk, locus_start, locus_end, locus_effects):
+    blocks = reach_blk.shape[0]
+    devices = lax.axis_size(("var", "smp", "sub"))
+    short = blocks * BLK == locus_effects.shape[1] and locus_start.shape[0] == devices
+    run = slab_body if short else wide_body
+    return run(dosages, reach_blk, locus_start, locus_end, locus_effects)
+
+
 def solution(mesh):
     in_specs = (
         P(("smp", "sub"), ("grp", "var")),

time: 227 us -> 27 us (0.12)
  waiting for transfers between devices: 122 us -> 0 us
  blocking collectives: 73.9 us -> 0 us
  Pallas kernels: 0 us -> 22.6 us
  between operations: 13.6 us -> 0.01 us
  matrix products: 5.4 us -> 0 us
  starting transfers between devices: 4.54 us -> 0 us
  other arithmetic: 2.79 us -> 0 us
    unnamed x2 -> x0, waiting for transfers between devices: 122 us -> none
    all_gather x1 -> x0, blocking collectives: 49.6 us -> none  [body(): lax.all_gather(locus_effects, ('var', 'smp', 'sub'), axis=0, tiled=True)]
    psum x2 -> x0, blocking collectives: 24.3 us -> none  [the longest x1 12.2 us: body(): lax.psum(jnp.sum(window, axis=0, dtype=jnp.float32), ('smp', 'sub'))]
    pallas_call x0 -> x1, Pallas kernels: none -> 22.6 us  [slab_body(): pl.pallas_call(functools.partial(kernel, n_var, n_smp, n_sub), out_shape=...]
    dot_general x5 -> x0, matrix products: 5.4 us -> none  [the longest x1 1.9 us: body(): y_cols = jnp.dot(b_rows, strict, precision=HIGHEST)]
    ppermute x4 -> x0, starting transfers between devices: 4.53 us -> none  [shifted(): return lax.ppermute(block, axis, route)]
  transfers between devices with their start and end apart: 5 -> 0, of which waited for: 1 -> 0; matrix products, arithmetic and copies ran while one was open for 2% -> 0% of each run, Pallas kernels for 0% -> 0%
where the time goes in v1:
time: 27 us; the launch traced here: 26.8 us
  Pallas kernels  22.6 us (84%)
  local copies, waits for them, and re-layouts  4.2 us (16%)
    pallas_call x1, Pallas kernels, slab_body(): pl.pallas_call(functools.partial(kernel, n_var, n_smp, n_sub), out_shape=...  22.6 us
    unnamed x11, local copies, waits for them, and re-layouts  4.2 us

profile of v1, /device:TPU:0, one launch (start us, length us, event | category | flops | bytes accessed | tf_op | source)
XLA Modules:
  0.0 26.8 jit_solution(458144858221934765)
XLA Ops:
  0.0 0.0 copy-start
  0.0 0.9 %copy-done = bf16[512,256]{1,0:T(8,128)(2,1)S(1)} copy-done((bf16[512,256]{1,0:T(8,128)(2,1)S(1)}, bf16[512,256]{1,0:T(8,128)(2,1)}, u32[]{:S(2)}) %copy-start) | copy-done | bytes 262168
  1.0 0.0 copy-start.1
  1.0 0.7 %copy-done.1 = bf16[1,1024]{1,0:T(2,128)(2,1)S(1)} copy-done((bf16[1,1024]{1,0:T(2,128)(2,1)S(1)}, bf16[1,1024]{1,0:T(2,128)(2,1)}, u32[]{:S(2)}) %copy-start.1) | copy-done | bytes 2072
  1.6 0.0 copy-start.2
  1.6 0.7 %copy-done.2 = s32[8]{0:T(128)S(1)} copy-done((s32[8]{0:T(128)S(1)}, s32[8]{0:T(128)}, u32[]{:S(2)}) %copy-start.2) | copy-done | bytes 56
  2.3 0.0 copy-start.3
  2.3 0.7 %copy-done.3 = s32[32]{0:T(128)S(1)} copy-done((s32[32]{0:T(128)S(1)}, s32[32]{0:T(128)}, u32[]{:S(2)}) %copy-start.3) | copy-done | bytes 152
  3.0 0.0 copy-start.4
  3.0 0.7 %copy-done.4 = s32[32]{0:T(128)S(1)} copy-done((s32[32]{0:T(128)S(1)}, s32[32]{0:T(128)}, u32[]{:S(2)}) %copy-start.4) | copy-done | bytes 152
  3.6 22.6 %shard_map.55 = f32[1,1024]{1,0:T(1,128)S(1)} custom-call(bf16[512,256]{1,0:T(8,128)(2,1)S(1)} %copy-done, s32[8]{0:T(128)S(1)} %copy-done.2, s32[32]{0:T(128)S(1)} %copy-done.3, s32[32]{0:T(128)S(1)} %copy-done.4, bf16[1,1024]{1,0:T(2,128)(2,1)S(1)} %copy-done.1), custom_call_target="tpu_custom_call" | custom-call | tf_op jit(solution)/shard_map/pallas_call | solution.py:272
  26.2 0.6 %copy.7 = f32[1,1024]{1,0:T(1,128)} copy(f32[1,1024]{1,0:T(1,128)S(1)} %shard_map.55) | data formatting | bytes 8192
Async XLA Ops:
  0.0 0.9 %copy-start = (bf16[512,256]{1,0:T(8,128)(2,1)S(1)}, bf16[512,256]{1,0:T(8,128)(2,1)}, u32[]{:S(2)}) copy-start(bf16[512,256]{1,0:T(8,128)(2,1)} %dos_any.1) | copy-start | bytes 786436
  1.0 0.7 %copy-start.1 = (bf16[1,1024]{1,0:T(2,128)(2,1)S(1)}, bf16[1,1024]{1,0:T(2,128)(2,1)}, u32[]{:S(2)}) copy-start(bf16[1,1024]{1,0:T(2,128)(2,1)} %eff_ref.1) | copy-start | bytes 6148
  1.6 0.7 %copy-start.2 = (s32[8]{0:T(128)S(1)}, s32[8]{0:T(128)}, u32[]{:S(2)}) copy-start(s32[8]{0:T(128)} %reach.1) | copy-start | bytes 100
  2.3 0.7 %copy-start.3 = (s32[32]{0:T(128)S(1)}, s32[32]{0:T(128)}, u32[]{:S(2)}) copy-start(s32[32]{0:T(128)} %start.1) | copy-start | bytes 388
  3.0 0.7 %copy-start.4 = (s32[32]{0:T(128)S(1)}, s32[32]{0:T(128)}, u32[]{:S(2)}) copy-start(s32[32]{0:T(128)} %end.1) | copy-start | bytes 388

commit v2 on v1

--- a/solution.py
+++ b/solution.py
@@ -113,10 +113,10 @@
     return jnp.concatenate([high, low], axis=0)
 
 
-def kernel(n_var, n_smp, n_sub, dos_any, reach, start, end, eff_ref, out_ref,
-           local, x, st, ms, e, y, ry, rs, rz,
-           local_sem, x_s, x_r, st_s, st_r, ms_s, ms_r, e1_s, e1_r, e2_s, e2_r,
-           ry_s, ry_r, rz_s, rz_r):
+def kernel(n_var, n_smp, n_sub, dos_any, reach_any, start_any, end_any, eff_any, out_ref,
+           reach, start, end, eff_ref, local, x, st, ms, e, y, ry,
+           small_sem, local_sem, x_s, x_r, st_s, st_r, ms_s, ms_r, e1_s, e1_r, e2_s, e2_r,
+           ry_s, ry_r):
     n_pl = n_smp * n_sub
     rows, stripe = dos_any.shape
     part = rows // n_var
@@ -135,6 +135,11 @@
         q = lax.rem(p + d, n_pl)
         return q, {"smp": lax.div(q, n_sub), "sub": lax.rem(q, n_sub)}
 
+    def any_peer(d):
+        g = lax.rem(p * n_var + v + d, loci)
+        q = lax.div(g, n_var)
+        return g, {"var": lax.rem(g, n_var), "smp": lax.div(q, n_sub), "sub": lax.rem(q, n_sub)}
+
     def rows_of(index, count):
         return pl.ds(pl.multiple_of(index * count, count), count)
 
@@ -145,17 +150,21 @@
         copy.start()
         return copy
 
+    small = [pltpu.make_async_copy(src, dst, small_sem.at[n]) for n, (src, dst) in enumerate((
+        (eff_any, eff_ref), (start_any, start), (end_any, end), (reach_any, reach)))]
+    for copy in small:
+        copy.start()
     whole = pltpu.make_async_copy(dos_any, local, local_sem.at[0])
     whole.start()
     own = pltpu.make_async_copy(dos_any.at[rows_of(v, part), :], x.at[v], local_sem.at[1])
     own.start()
 
     barrier = pltpu.get_barrier_semaphore()
-    for d in range(1, n_var):
-        pl.semaphore_signal(barrier, inc=1, device_id=var_peer(d)[1], device_id_type=MESH)
-    for d in range(1, n_pl):
-        pl.semaphore_signal(barrier, inc=1, device_id=plane_peer(d)[1], device_id_type=MESH)
-
+    for d in range(1, loci):
+        pl.semaphore_signal(barrier, inc=1, device_id=any_peer(d)[1], device_id_type=MESH)
+
+    for copy in small:
+        copy.wait()
     me = v * n_pl + p
     first, last = start[me], end[me]
     block_row = lax.broadcasted_iota(jnp.int32, (blocks, BLK), 0)
@@ -167,7 +176,7 @@
     own_rows = rows_of(p * n_var + v, blocks)
     e[own_rows, :] = placed
 
-    pl.semaphore_wait(barrier, n_var - 1 + n_pl - 1)
+    pl.semaphore_wait(barrier, loci - 1)
     e1 = [send(e.at[own_rows, :], e.at[own_rows, :], e1_s.at[d], e1_r.at[d], var_peer(d)[1])
           for d in range(1, n_var)]
     xs = []
@@ -200,7 +209,9 @@
     for q in range(n_pl):
         spread = spread + (st[q, 1:2, :] + rows * jnp.square(st[q, 0:1, :] / rows - mean))
     ms[v, 0:1, :] = mean
-    ms[v, 1:2, :] = lax.rsqrt(spread / samples + EPS)
+    var_eps = spread / samples + EPS
+    inv = lax.rsqrt(var_eps)
+    ms[v, 1:2, :] = inv * (1.5 - 0.5 * var_eps * inv * inv)
     mss = [send(ms.at[v], ms.at[v], ms_s.at[d], ms_r.at[d], var_peer(d)[1])
            for d in range(1, n_var)]
     for copy in e2:
@@ -233,27 +244,16 @@
                             preferred_element_type=jnp.float32)
         y[pl.ds(i, loci, stride=blocks), :] = (r[:loci] + r[loci:]) * (ms[s, 1:2, c] / samples)
 
-    rys = []
-    for d in range(1, n_pl):
-        q, peer = plane_peer(d)
-        rys.append(send(y.at[rows_of(q, n_var * blocks), :], ry.at[p], ry_s.at[d], ry_r.at[d], peer))
-    ry[p] = y[group, :]
-    for copy in rys:
-        copy.wait()
-    acc = ry[0]
-    for q in range(1, n_pl):
-        acc = acc + ry[q]
-    rs[...] = acc
-    rzs = []
-    for d in range(1, n_var):
-        t, peer = var_peer(d)
-        rzs.append(send(rs.at[rows_of(t, blocks), :], rz.at[v], rz_s.at[d], rz_r.at[d], peer))
-    rz[v] = rs[rows_of(v, blocks), :]
-    for copy in rzs:
-        copy.wait()
-    score = rz[0]
-    for t in range(1, n_var):
-        score = score + rz[t]
+    for d in range(1, loci):
+        g, peer = any_peer(d)
+        send(y.at[rows_of(g, blocks), :], ry.at[d], ry_s.at[0], ry_r.at[0], peer)
+    score = y[own_rows, :]
+    sent = y.at[pl.ds(0, (loci - 1) * blocks), :]
+    landed = ry.at[pl.ds(1, loci - 1)]
+    pltpu.make_async_copy(sent, sent, ry_s.at[0]).wait()
+    pltpu.make_async_copy(landed, landed, ry_r.at[0]).wait()
+    for d in range(1, loci):
+        score = score + ry[d]
     for k in range(eff.shape[1] // BLK):
         hit = (block_row == first + k) & (block_row <= last)
         out_ref[:, k * BLK:(k + 1) * BLK] = jnp.sum(jnp.where(hit, score, 0.0), axis=0, keepdims=True)
@@ -267,34 +267,35 @@
     loci = locus_start.shape[0]
     f32 = jnp.float32
     dma = pltpu.SemaphoreType.DMA
-    smem = pl.BlockSpec(memory_space=pltpu.SMEM)
+    hbm = pl.BlockSpec(memory_space=pltpu.HBM)
     vmem = pl.BlockSpec(memory_space=pltpu.VMEM)
     return pl.pallas_call(
         functools.partial(kernel, n_var, n_smp, n_sub),
         out_shape=jax.ShapeDtypeStruct(locus_effects.shape, f32),
-        in_specs=[pl.BlockSpec(memory_space=pl.ANY), smem, smem, smem, vmem],
+        in_specs=[hbm] * 5,
         out_specs=vmem,
         scratch_shapes=[
+            pltpu.SMEM(reach_blk.shape, reach_blk.dtype),
+            pltpu.SMEM(locus_start.shape, locus_start.dtype),
+            pltpu.SMEM(locus_end.shape, locus_end.dtype),
+            pltpu.VMEM(locus_effects.shape, locus_effects.dtype),
             pltpu.VMEM((rows, stripe), dosages.dtype),
             pltpu.VMEM((n_var, rows // n_var, stripe), dosages.dtype),
             pltpu.VMEM((n_pl, 2, stripe), f32),
             pltpu.VMEM((n_var, 2, stripe), f32),
             pltpu.VMEM((loci * blocks, BLK), f32),
             pltpu.VMEM((loci * blocks, BLK), f32),
-            pltpu.VMEM((n_pl, n_var * blocks, BLK), f32),
-            pltpu.VMEM((n_var * blocks, BLK), f32),
-            pltpu.VMEM((n_var, blocks, BLK), f32),
-            dma((2,)),
+            pltpu.VMEM((loci, blocks, BLK), f32),
+            dma((4,)), dma((2,)),
             dma((n_var,)), dma((n_var,)),
             dma((n_pl,)), dma((n_pl,)),
             dma((n_var,)), dma((n_var,)),
             dma((n_var,)), dma((n_var,)),
             dma((n_pl,)), dma((n_pl,)),
-            dma((n_pl,)), dma((n_pl,)),
-            dma((n_var,)), dma((n_var,)),
+            dma((1,)), dma((1,)),
         ],
         compiler_params=pltpu.CompilerParams(
-            collective_id=0, has_side_effects=True, vmem_limit_bytes=16 * 1024 * 1024),
+            collective_id=0, has_side_effects=True, vmem_limit_bytes=60 * 1024 * 1024),
     )(dosages, reach_blk, locus_start, locus_end, locus_effects)
 
 

time: 27 us -> 22.9 us (0.85)
  local copies, waits for them, and re-layouts: 4.2 us -> 1.28 us
  Pallas kernels: 22.6 us -> 21.5 us
    unnamed x11 -> x1, local copies, waits for them, and re-layouts: 4.2 us -> 1.28 us
    pallas_call x1, Pallas kernels: 22.6 us -> 21.5 us  [slab_body(): pl.pallas_call(functools.partial(kernel, n_var, n_smp, n_sub), out_shape=...]
where the time goes in v2:
time: 22.9 us; the launch traced here: 22.7 us
  Pallas kernels  21.5 us (94%)
  local copies, waits for them, and re-layouts  1.28 us (6%)
    pallas_call x1, Pallas kernels, slab_body(): pl.pallas_call(functools.partial(kernel, n_var, n_smp, n_sub), out_shape=...  21.5 us
    unnamed x1, local copies, waits for them, and re-layouts  1.28 us

profile of v2, /device:TPU:0, one launch (start us, length us, event | category | flops | bytes accessed | tf_op | source)
XLA Modules:
  0.0 22.7 jit_solution(1776276524577179243)
XLA Ops:
  0.0 21.5 %shard_map.55 = f32[1,1024]{1,0:T(1,128)} custom-call(bf16[512,256]{1,0:T(8,128)(2,1)} %dos_any.1, s32[8]{0:T(128)} %reach_any.1, s32[32]{0:T(128)} %start_any.1, s32[32]{0:T(128)} %end_any.1, bf16[1,1024]{1,0:T(2,128)(2,1)} %eff_any.1), custom_call_target="tpu_custom_call" | custom-call | tf_op jit(solution)/shard_map/pallas_call | solution.py:272
  21.5 1.3 %copy.7 = f32[1,1024]{1,0:T(1,128)} copy(f32[1,1024]{1,0:T(1,128)} %shard_map.55) | data formatting | bytes 8192

commit v3 on v2

--- a/solution.py
+++ b/solution.py
@@ -113,6 +113,11 @@
     return jnp.concatenate([high, low], axis=0)
 
 
+def rejoined(pair):
+    half = pair.shape[0] // 2
+    return pair[:half].astype(jnp.float32) + pair[half:].astype(jnp.float32)
+
+
 def kernel(n_var, n_smp, n_sub, dos_any, reach_any, start_any, end_any, eff_any, out_ref,
            reach, start, end, eff_ref, local, x, st, ms, e, y, ry,
            small_sem, local_sem, x_s, x_r, st_s, st_r, ms_s, ms_r, e1_s, e1_r, e2_s, e2_r,
@@ -150,6 +155,10 @@
         copy.start()
         return copy
 
+    barrier = pltpu.get_barrier_semaphore()
+    for d in range(1, loci):
+        pl.semaphore_signal(barrier, inc=1, device_id=any_peer(d)[1], device_id_type=MESH)
+
     small = [pltpu.make_async_copy(src, dst, small_sem.at[n]) for n, (src, dst) in enumerate((
         (eff_any, eff_ref), (start_any, start), (end_any, end), (reach_any, reach)))]
     for copy in small:
@@ -158,10 +167,6 @@
     whole.start()
     own = pltpu.make_async_copy(dos_any.at[rows_of(v, part), :], x.at[v], local_sem.at[1])
     own.start()
-
-    barrier = pltpu.get_barrier_semaphore()
-    for d in range(1, loci):
-        pl.semaphore_signal(barrier, inc=1, device_id=any_peer(d)[1], device_id_type=MESH)
 
     for copy in small:
         copy.wait()
@@ -176,22 +181,21 @@
     own_rows = rows_of(p * n_var + v, blocks)
     e[own_rows, :] = placed
 
-    pl.semaphore_wait(barrier, loci - 1)
-    e1 = [send(e.at[own_rows, :], e.at[own_rows, :], e1_s.at[d], e1_r.at[d], var_peer(d)[1])
-          for d in range(1, n_var)]
-    xs = []
-    for d in range(1, n_var):
-        t, peer = var_peer(d)
-        xs.append(send(dos_any.at[rows_of(t, part), :], x.at[v], x_s.at[d], x_r.at[d], peer))
-
     whole.wait()
     mine = local[...].astype(jnp.float32)
     total = jnp.sum(mine, axis=0, keepdims=True)
     sq = jnp.sum(jnp.square(mine - total / rows), axis=0, keepdims=True)
     st[p, 0:1, :] = total
     st[p, 1:2, :] = sq
+    pl.semaphore_wait(barrier, loci - 1)
+    e1 = [send(e.at[own_rows, :], e.at[own_rows, :], e1_s.at[d], e1_r.at[d], var_peer(d)[1])
+          for d in range(1, n_var)]
     sts = [send(st.at[p], st.at[p], st_s.at[d], st_r.at[d], plane_peer(d)[1])
            for d in range(1, n_pl)]
+    xs = []
+    for d in range(1, n_var):
+        t, peer = var_peer(d)
+        xs.append(send(dos_any.at[rows_of(t, part), :], x.at[v], x_s.at[d], x_r.at[d], peer))
 
     for copy in e1:
         copy.wait()
@@ -229,9 +233,10 @@
     for j in range(blocks):
         s, c = cols(j)
         z = e[pl.ds(j, loci, stride=blocks), :] * ms[s, 1:2, c]
-        w = lax.dot_general(halves(z), x[s, :, c], (((1,), (1,)), ((), ())),
+        pair = halves(z)
+        w = lax.dot_general(pair, x[s, :, c], (((1,), (1,)), ((), ())),
                             preferred_element_type=jnp.float32)
-        shift = jnp.sum(z * ms[s, 0:1, c], axis=1, keepdims=True)
+        shift = jnp.sum(rejoined(pair) * ms[s, 0:1, c], axis=1, keepdims=True)
         parts.append(w[:loci] + w[loci:] - shift)
     for i in range(blocks):
         s, c = cols(i)

time: 22.9 us -> 22.9 us (level)
  no operation moved by 1% of the time
where the time goes in v3:
time: 22.9 us; the launch traced here: 22.7 us
  Pallas kernels  21.4 us (93%)
  local copies, waits for them, and re-layouts  1.28 us (6%)
    pallas_call x1, Pallas kernels, slab_body(): pl.pallas_call(functools.partial(kernel, n_var, n_smp, n_sub), out_shape=...  21.4 us
    unnamed x1, local copies, waits for them, and re-layouts  1.28 us

profile of v3, /device:TPU:0, one launch (start us, length us, event | category | flops | bytes accessed | tf_op | source)
XLA Modules:
  0.0 22.7 jit_solution(2753697678380669863)
XLA Ops:
  0.0 21.4 %shard_map.55 = f32[1,1024]{1,0:T(1,128)} custom-call(bf16[512,256]{1,0:T(8,128)(2,1)} %dos_any.1, s32[8]{0:T(128)} %reach_any.1, s32[32]{0:T(128)} %start_any.1, s32[32]{0:T(128)} %end_any.1, bf16[1,1024]{1,0:T(2,128)(2,1)} %eff_any.1), custom_call_target="tpu_custom_call" | custom-call | tf_op jit(solution)/shard_map/pallas_call | solution.py:277
  21.4 1.3 %copy.7 = f32[1,1024]{1,0:T(1,128)} copy(f32[1,1024]{1,0:T(1,128)} %shard_map.55) | data formatting | bytes 8192

commit v4 on v3

--- a/solution.py
+++ b/solution.py
@@ -238,20 +238,32 @@
                             preferred_element_type=jnp.float32)
         shift = jnp.sum(rejoined(pair) * ms[s, 0:1, c], axis=1, keepdims=True)
         parts.append(w[:loci] + w[loci:] - shift)
+    bands = []
     for i in range(blocks):
-        s, c = cols(i)
         summed = parts[i]
         for j in range(blocks):
             if j != i:
                 low, high = min(i, j), max(i, j)
                 summed = summed + jnp.where(reach[low] >= high - low, 1.0, 0.0) * parts[j]
-        r = lax.dot_general(halves(summed), x[s, :, c], (((1,), (0,)), ((), ())),
-                            preferred_element_type=jnp.float32)
-        y[pl.ds(i, loci, stride=blocks), :] = (r[:loci] + r[loci:]) * (ms[s, 1:2, c] / samples)
-
-    for d in range(1, loci):
-        g, peer = any_peer(d)
-        send(y.at[rows_of(g, blocks), :], ry.at[d], ry_s.at[0], ry_r.at[0], peer)
+        bands.append(summed)
+    half = loci // 2
+    here = p * n_var + v
+    for group_of in range(2):
+        base = group_of * half
+        for i in range(blocks):
+            s, c = cols(i)
+            r = lax.dot_general(halves(bands[i][base:base + half]), x[s, :, c],
+                                (((1,), (0,)), ((), ())), preferred_element_type=jnp.float32)
+            y[pl.ds(base * blocks + i, half, stride=blocks), :] = (
+                r[:half] + r[half:]) * (ms[s, 1:2, c] / samples)
+        for g in range(base, base + half):
+            q = g // n_var
+            peer = {"var": g % n_var, "smp": q // n_sub, "sub": q % n_sub}
+
+            @pl.when(here != g)
+            def _():
+                send(y.at[pl.ds(g * blocks, blocks), :], ry.at[lax.rem(g - here + loci, loci)],
+                     ry_s.at[0], ry_r.at[0], peer)
     score = y[own_rows, :]
     sent = y.at[pl.ds(0, (loci - 1) * blocks), :]
     landed = ry.at[pl.ds(1, loci - 1)]

time: 22.9 us -> 22.1 us (0.965)
  Pallas kernels: 21.4 us -> 20.6 us
    pallas_call x1, Pallas kernels: 21.4 us -> 20.6 us  [slab_body(): pl.pallas_call(functools.partial(kernel, n_var, n_smp, n_sub), out_shape=...]
where the time goes in v4:
time: 22.1 us; the launch traced here: 21.9 us
  Pallas kernels  20.6 us (93%)
  local copies, waits for them, and re-layouts  1.28 us (6%)
    pallas_call x1, Pallas kernels, slab_body(): pl.pallas_call(functools.partial(kernel, n_var, n_smp, n_sub), out_shape=...  20.6 us
    unnamed x1, local copies, waits for them, and re-layouts  1.28 us

profile of v4, /device:TPU:0, one launch (start us, length us, event | category | flops | bytes accessed | tf_op | source)
XLA Modules:
  0.0 21.9 jit_solution(14722690592604715117)
XLA Ops:
  0.0 20.6 %shard_map.55 = f32[1,1024]{1,0:T(1,128)} custom-call(bf16[512,256]{1,0:T(8,128)(2,1)} %dos_any.1, s32[8]{0:T(128)} %reach_any.1, s32[32]{0:T(128)} %start_any.1, s32[32]{0:T(128)} %end_any.1, bf16[1,1024]{1,0:T(2,128)(2,1)} %eff_any.1), custom_call_target="tpu_custom_call" | custom-call | tf_op jit(solution)/shard_map/pallas_call | solution.py:289
  20.6 1.3 %copy.7 = f32[1,1024]{1,0:T(1,128)} copy(f32[1,1024]{1,0:T(1,128)} %shard_map.55) | data formatting | bytes 8192
